TPU v7x, 32 devices: a whole 2x2x4 slice. The times are simulated.
32 devices in a mesh: cell: 2 (over core), gene: 16 (over z, y, x).
Axes of the slice: x: 2, y: 2, z: 4, core: 2. Of those that a mesh axis runs over, the one named last changes fastest.
Arguments:
- encoder_packed_tokens: bfloat16 [2, 15360, 768], P('cell', 'gene'), may hold values from -6 to 6
- token_gene_index: int32 [2, 15360], P('cell', 'gene'), may hold values from -1 to 2559, as said below
- cell_counts: int32 [2, 128], P('cell', 'gene'), may hold values from 40 to 120
- zero_embed: bfloat16 [2560, 768], P('gene'), may hold values from -6 to 6
- random_features: bfloat16 [64, 256], replicated, may hold values from -4 to 4
- input_weight: bfloat16 [768, 512], replicated, may hold values from -0.21875 to 0.21875
- input_bias: float32 [512], replicated, may hold values from -0.15625 to 0.15625
- first_gain: float32 [512], replicated, may hold values from 0.5 to 1.5
- first_shift: float32 [512], replicated, may hold values from -0.15625 to 0.15625
- joint_weight: bfloat16 [512, 1536], replicated, may hold values from -0.25 to 0.25
- joint_bias: float32 [1536], replicated, may hold values from -0.15625 to 0.15625
- output_weight: bfloat16 [512, 512], replicated, may hold values from -1.5 to 1.5
- output_bias: float32 [512], replicated, may hold values from -4 to 4
- second_gain: float32 [512], replicated, may hold values from 0.5 to 1.5
- second_shift: float32 [512], replicated, may hold values from -4 to 4
- upper_weight: bfloat16 [512, 2048], replicated, may hold values from -0.25 to 0.25
- upper_bias: float32 [2048], replicated, may hold values from -4 to 4
- lower_weight: bfloat16 [2048, 512], replicated, may hold values from -0.125 to 0.125
- lower_bias: float32 [512], replicated, may hold values from -4 to 4
- cotangent: bfloat16 [16, 2560, 512], P('cell', 'gene'), may hold values from -6 to 6
Outputs:
- block_out: bfloat16 [16, 2560, 512], P('cell', 'gene')
- token_grad: float32 [2, 15360, 768], P('cell', 'gene')
- zero_grad: float32 [2560, 768], P('gene')
- grad_input_weight: float32 [768, 512], P('gene')
- grad_input_bias: float32 [512], P('gene')
- grad_first_gain: float32 [512], P('gene')
- grad_first_shift: float32 [512], P('gene')
- grad_joint_weight: float32 [512, 1536], P('gene')
- grad_joint_bias: float32 [1536], P('gene')
- grad_output_weight: float32 [512, 512], P('gene')
- grad_output_bias: float32 [512], P('gene')
- grad_second_gain: float32 [512], P('gene')
- grad_second_shift: float32 [512], P('gene')
- grad_upper_weight: float32 [512, 2048], P('gene')
- grad_upper_bias: float32 [2048], P('gene')
- grad_lower_weight: float32 [2048, 512], P('gene')
- grad_lower_bias: float32 [512], P('gene')
Inputs may be any that keep to these rules, and one draw needn't show every extreme that they name: `token_gene_index`: row (a, s) holds only genes of s * 160 to (s + 1) * 160 - 1; each cell's genes in a row are distinct and ascending; the empty slots after the row's tokens hold -1.
All inputs are finite; a program needn't handle non-finite values.
Results may differ from a plain program's by a relative error of at most 0.019.
Values sent between devices are 32-bit elements; how exact they have to be, the bound alone decides.
No kernel may reach another device: no remote copies, remote signals or barrier semaphores. Data moves between devices by JAX's collectives and lax.ppermute only.
A program may use at most 192 MiB of HBM per device.

v0:
```python
import jax
import jax.numpy as jnp
from jax import lax
from jax.sharding import PartitionSpec as P

epsilon = 1e-05
highest = lax.Precision.HIGHEST


def normalize(values, gain_vector, shift_vector):
    centred = values - jnp.mean(values, axis=-1, keepdims=True)
    inverse = lax.rsqrt(jnp.mean(centred * centred, axis=-1, keepdims=True) + epsilon)
    scaled = centred * inverse
    return (scaled * gain_vector + shift_vector, scaled, inverse)


def normalize_back(grad_in, scaled, inverse, gain_vector):
    weighted = grad_in * gain_vector
    return inverse * (
        weighted
        - jnp.mean(weighted, axis=-1, keepdims=True)
        - scaled * jnp.mean(weighted * scaled, axis=-1, keepdims=True)
    )


def feature_map(heads_in, random_features, factor):
    projected = jnp.einsum(
        "cghd,dm->cghm", heads_in, random_features, preferred_element_type=jnp.float32
    )
    widened = heads_in.astype(jnp.float32)
    squared = jnp.sum(widened * widened, axis=-1, keepdims=True)
    feature_count = random_features.shape[1]
    return jnp.exp(factor * projected - 0.5 * factor * factor * squared) * feature_count ** (-0.5)


def feature_back(grad_feat, feature_values, heads_in, random_features, factor):
    weighted = grad_feat * feature_values
    projected_grad = (weighted * factor).astype(jnp.bfloat16)
    through = jnp.einsum(
        "cghm,dm->cghd", projected_grad, random_features, preferred_element_type=jnp.float32
    )
    return through - factor * factor * heads_in.astype(jnp.float32) * jnp.sum(
        weighted, axis=-1, keepdims=True
    )


def forward_pass(gene_rows, weights, reducer):
    (
        random_features,
        input_weight,
        input_bias,
        first_gain,
        first_shift,
        joint_weight,
        joint_bias,
        output_weight,
        output_bias,
        second_gain,
        second_shift,
        upper_weight,
        upper_bias,
        lower_weight,
        lower_bias,
    ) = weights
    cells_here, device_genes, width_in = gene_rows.shape
    width = input_weight.shape[1]
    head_size = random_features.shape[0]
    head_count = width // head_size
    factor = head_size ** (-0.25)
    flat_rows = gene_rows.reshape(cells_here * device_genes, width_in)
    hidden = jnp.dot(flat_rows, input_weight, preferred_element_type=jnp.float32) + input_bias
    normed, scaled_one, inverse_one = normalize(hidden, first_gain, first_shift)
    normed_low = normed.astype(jnp.bfloat16)
    joint = (
        jnp.dot(normed_low, joint_weight, preferred_element_type=jnp.float32) + joint_bias
    ).astype(jnp.bfloat16)
    split_shape = (cells_here, device_genes, head_count, head_size)
    query = joint[:, :width].reshape(split_shape)
    key_part = joint[:, width : 2 * width].reshape(split_shape)
    value_portion = joint[:, 2 * width :].reshape(split_shape)
    query_features = feature_map(query, random_features, factor)
    key_features = feature_map(key_part, random_features, factor)
    query_low = query_features.astype(jnp.bfloat16)
    key_low = key_features.astype(jnp.bfloat16)
    local_summary = jnp.einsum(
        "cghm,cghd->chmd", key_low, value_portion, preferred_element_type=jnp.float32
    )
    local_total = jnp.sum(key_low, axis=1, dtype=jnp.float32)
    key_value_summary, total = reducer(local_summary, local_total)
    query_wide = query_low.astype(jnp.float32)
    attention_numerator = jnp.einsum(
        "cghm,chmd->cghd", query_wide, key_value_summary, precision=highest
    )
    denominator = jnp.einsum("cghm,chm->cgh", query_wide, total, precision=highest)
    attention = attention_numerator / denominator[..., None]
    attention_low = attention.reshape(cells_here * device_genes, width).astype(jnp.bfloat16)
    middle = hidden + (
        jnp.dot(attention_low, output_weight, preferred_element_type=jnp.float32) + output_bias
    )
    normed_two, scaled_two, inverse_two = normalize(middle, second_gain, second_shift)
    normed_two_low = normed_two.astype(jnp.bfloat16)
    upper = jnp.dot(normed_two_low, upper_weight, preferred_element_type=jnp.float32) + upper_bias
    active_low = jax.nn.gelu(upper, approximate=False).astype(jnp.bfloat16)
    result = middle + (
        jnp.dot(active_low, lower_weight, preferred_element_type=jnp.float32) + lower_bias
    )
    saved = (
        flat_rows,
        scaled_one,
        inverse_one,
        normed_low,
        value_portion,
        query,
        key_part,
        query_features,
        key_features,
        query_low,
        query_wide,
        key_low,
        key_value_summary,
        total,
        denominator,
        attention,
        attention_low,
        scaled_two,
        inverse_two,
        normed_two_low,
        upper,
        active_low,
    )
    return (result, saved)


def local(
    encoder_packed_tokens,
    token_gene_index,
    cell_counts,
    zero_embed,
    random_features,
    input_weight,
    input_bias,
    first_gain,
    first_shift,
    joint_weight,
    joint_bias,
    output_weight,
    output_bias,
    second_gain,
    second_shift,
    upper_weight,
    upper_bias,
    lower_weight,
    lower_bias,
    cotangent,
):
    weights = (
        random_features,
        input_weight,
        input_bias,
        first_gain,
        first_shift,
        joint_weight,
        joint_bias,
        output_weight,
        output_bias,
        second_gain,
        second_shift,
        upper_weight,
        upper_bias,
        lower_weight,
        lower_bias,
    )
    cells_here, device_genes, width = cotangent.shape
    row_length = encoder_packed_tokens.shape[1]
    width_in = encoder_packed_tokens.shape[2]
    token_count = cells_here * device_genes
    head_size = random_features.shape[0]
    factor = head_size ** (-0.25)
    first_gene = lax.axis_index("gene") * device_genes
    cell_ends = jnp.cumsum(cell_counts[0])
    slot_indices = jnp.arange(row_length, dtype=jnp.int32)
    segment = jnp.sum((slot_indices[:, None] >= cell_ends[None, :]).astype(jnp.int32), axis=1)
    living = segment < cells_here
    target_slot = jnp.where(living, segment * device_genes + token_gene_index[0] - first_gene, -1)
    places = jnp.arange(token_count, dtype=jnp.int32)
    select = target_slot[:, None] == places[None, :]
    scattered_tokens = jnp.einsum(
        "rt,ri->ti",
        select.astype(jnp.bfloat16),
        encoder_packed_tokens[0],
        preferred_element_type=jnp.float32,
    )
    vacant = 1.0 - jnp.sum(select.astype(jnp.float32), axis=0)
    gene_rows = scattered_tokens + vacant[:, None] * jnp.tile(
        zero_embed.astype(jnp.float32), (cells_here, 1)
    )
    gene_rows = gene_rows.astype(jnp.bfloat16).reshape(cells_here, device_genes, width_in)
    output, saved = forward_pass(
        gene_rows, weights, lambda summary_in, total_in: lax.psum((summary_in, total_in), "gene")
    )
    discard, saved = forward_pass(
        gene_rows, weights, lambda summary_in, total_in: lax.psum((summary_in, total_in), "gene")
    )
    (
        flat_rows,
        scaled_one,
        inverse_one,
        normed_low,
        value_portion,
        query,
        key_part,
        query_features,
        key_features,
        query_low,
        query_wide,
        key_low,
        key_value_summary,
        total,
        denominator,
        attention,
        attention_low,
        scaled_two,
        inverse_two,
        normed_two_low,
        upper,
        active_low,
    ) = saved
    grad_low = cotangent.reshape(token_count, width)
    grad_out = grad_low.astype(jnp.float32)
    grad_lower_weight = jnp.einsum(
        "tf,td->fd", active_low, grad_low, preferred_element_type=jnp.float32
    )
    grad_lower_bias = jnp.sum(grad_out, axis=0)
    grad_active = jnp.einsum(
        "td,fd->tf", grad_low, lower_weight, preferred_element_type=jnp.float32
    )
    cumulative = 0.5 * (1.0 + lax.erf(upper * 0.7071067811865476))
    density = jnp.exp(-0.5 * upper * upper) * 0.3989422804014327
    upper_low = (grad_active * (cumulative + upper * density)).astype(jnp.bfloat16)
    grad_upper_weight = jnp.einsum(
        "td,tf->df", normed_two_low, upper_low, preferred_element_type=jnp.float32
    )
    grad_upper_bias = jnp.sum(upper_low, axis=0, dtype=jnp.float32)
    grad_normed_two = jnp.einsum(
        "tf,df->td", upper_low, upper_weight, preferred_element_type=jnp.float32
    )
    grad_second_gain = jnp.sum(grad_normed_two * scaled_two, axis=0)
    grad_second_shift = jnp.sum(grad_normed_two, axis=0)
    grad_middle = grad_out + normalize_back(grad_normed_two, scaled_two, inverse_two, second_gain)
    branch_low = grad_middle.astype(jnp.bfloat16)
    grad_output_weight = jnp.einsum(
        "te,td->ed", attention_low, branch_low, preferred_element_type=jnp.float32
    )
    grad_output_bias = jnp.sum(branch_low, axis=0, dtype=jnp.float32)
    grad_attention = jnp.einsum(
        "td,ed->te", branch_low, output_weight, preferred_element_type=jnp.float32
    ).reshape(attention.shape)
    numerator_low = (grad_attention / denominator[..., None]).astype(jnp.bfloat16)
    grad_denominator = -jnp.sum(grad_attention * attention, axis=-1) / denominator
    local_grad_summary = jnp.einsum(
        "cghm,cghd->chmd", query_low, numerator_low, preferred_element_type=jnp.float32
    )
    local_grad_total = jnp.einsum("cghm,cgh->chm", query_wide, grad_denominator, precision=highest)
    grad_summary, grad_total = lax.psum((local_grad_summary, local_grad_total), "gene")
    grad_query_feat = (
        jnp.einsum(
            "cghd,chmd->cghm",
            numerator_low.astype(jnp.float32),
            key_value_summary,
            precision=highest,
        )
        + grad_denominator[..., None] * total[:, None]
    )
    grad_key_feat = (
        jnp.einsum(
            "cghd,chmd->cghm", value_portion.astype(jnp.float32), grad_summary, precision=highest
        )
        + grad_total[:, None]
    )
    grad_value = jnp.einsum(
        "cghm,chmd->cghd", key_low.astype(jnp.float32), grad_summary, precision=highest
    )
    grad_query = feature_back(grad_query_feat, query_features, query, random_features, factor)
    grad_key = feature_back(grad_key_feat, key_features, key_part, random_features, factor)
    joint_low = jnp.concatenate(
        [
            grad_query.reshape(token_count, width),
            grad_key.reshape(token_count, width),
            grad_value.reshape(token_count, width),
        ],
        axis=1,
    ).astype(jnp.bfloat16)
    grad_joint_weight = jnp.einsum(
        "td,te->de", normed_low, joint_low, preferred_element_type=jnp.float32
    )
    grad_joint_bias = jnp.sum(joint_low, axis=0, dtype=jnp.float32)
    grad_normed = jnp.einsum(
        "te,de->td", joint_low, joint_weight, preferred_element_type=jnp.float32
    )
    grad_first_gain = jnp.sum(grad_normed * scaled_one, axis=0)
    grad_first_shift = jnp.sum(grad_normed, axis=0)
    hidden_low = (
        grad_middle + normalize_back(grad_normed, scaled_one, inverse_one, first_gain)
    ).astype(jnp.bfloat16)
    grad_input_weight = jnp.einsum(
        "ti,td->id", flat_rows, hidden_low, preferred_element_type=jnp.float32
    )
    grad_input_bias = jnp.sum(hidden_low, axis=0, dtype=jnp.float32)
    grad_rows = jnp.einsum(
        "td,id->ti", hidden_low, input_weight, preferred_element_type=jnp.float32
    )
    block_out = output.reshape(cells_here, device_genes, width).astype(jnp.bfloat16)
    safe_target = jnp.where(living, target_slot, 0)
    token_grad = (
        jnp.take(grad_rows, safe_target, axis=0) * living[:, None].astype(jnp.float32)
    ).reshape(1, row_length, width_in)
    zero_local = jnp.sum(
        (vacant[:, None] * grad_rows).reshape(cells_here, device_genes, width_in), axis=0
    )
    pieces = (
        lax.psum_scatter(grad_input_weight, "gene", scatter_dimension=0, tiled=True),
        lax.psum_scatter(grad_input_bias, "gene", scatter_dimension=0, tiled=True),
        lax.psum_scatter(grad_first_gain, "gene", scatter_dimension=0, tiled=True),
        lax.psum_scatter(grad_first_shift, "gene", scatter_dimension=0, tiled=True),
        lax.psum_scatter(grad_joint_weight, "gene", scatter_dimension=0, tiled=True),
        lax.psum_scatter(grad_joint_bias, "gene", scatter_dimension=0, tiled=True),
        lax.psum_scatter(grad_output_weight, "gene", scatter_dimension=0, tiled=True),
        lax.psum_scatter(grad_output_bias, "gene", scatter_dimension=0, tiled=True),
        lax.psum_scatter(grad_second_gain, "gene", scatter_dimension=0, tiled=True),
        lax.psum_scatter(grad_second_shift, "gene", scatter_dimension=0, tiled=True),
        lax.psum_scatter(grad_upper_weight, "gene", scatter_dimension=0, tiled=True),
        lax.psum_scatter(grad_upper_bias, "gene", scatter_dimension=0, tiled=True),
        lax.psum_scatter(grad_lower_weight, "gene", scatter_dimension=0, tiled=True),
        lax.psum_scatter(grad_lower_bias, "gene", scatter_dimension=0, tiled=True),
    )
    summed = lax.psum(
        (
            pieces[0],
            pieces[1],
            pieces[2],
            pieces[3],
            pieces[4],
            pieces[5],
            pieces[6],
            pieces[7],
            pieces[8],
            pieces[9],
            pieces[10],
            pieces[11],
            pieces[12],
            pieces[13],
            zero_local,
        ),
        "cell",
    )
    return (
        block_out,
        token_grad,
        summed[14],
        summed[0],
        summed[1],
        summed[2],
        summed[3],
        summed[4],
        summed[5],
        summed[6],
        summed[7],
        summed[8],
        summed[9],
        summed[10],
        summed[11],
        summed[12],
        summed[13],
    )


def solution(mesh):
    return jax.shard_map(
        local,
        mesh=mesh,
        in_specs=(
            P("cell", "gene", None),
            P("cell", "gene"),
            P("cell", "gene"),
            P("gene", None),
            P(),
            P(),
            P(),
            P(),
            P(),
            P(),
            P(),
            P(),
            P(),
            P(),
            P(),
            P(),
            P(),
            P(),
            P(),
            P("cell", "gene", None),
        ),
        out_specs=(
            P("cell", "gene", None),
            P("cell", "gene", None),
            P("gene", None),
            P("gene", None),
            P("gene"),
            P("gene"),
            P("gene"),
            P("gene", None),
            P("gene"),
            P("gene", None),
            P("gene"),
            P("gene"),
            P("gene"),
            P("gene", None),
            P("gene"),
            P("gene", None),
            P("gene"),
        ),
        check_vma=False,
    )
```

profile of v0, /device:TPU:0, one launch (start us, length us, event | category | flops | bytes accessed | tf_op | source)
XLA Modules:
  0.0 1136.1 jit_solution(2646011942369654866)
XLA Ops:
  11.2 4.4 fusion.36
  21.9 4.3 reshape.306
  26.2 4.5 copy.97
  30.8 4.3 reshape.305
  35.1 3.4 fusion.20
  38.5 6.8 convert_reduce_fusion.1
  45.3 3.6 fusion.33
  51.9 3.4 fusion.23
  56.1 6.7 fusion.18
  62.8 160.2 %all-reduce.20.cloned.1.call-done = (f32[8,8,256]{2,1,0:T(8,128)}, f32[8,8,256,64]{2,3,1,0:T(8,128)}) async-done(((f32[8,8,256]{2,1,0:T(8,128)}, f32[8,8,256,64]{2,3,1,0:T(8,128)}), (f32[8,8,256]{2,1,0:T(8,128)}, f32[8,8,256,64]{2,3,1,0:T(8,128)})) %all-reduce.20.cloned.1.call-update) | async-done | bytes 4259856 | tf_op jit(solution)/shard_map/psum | solution.py:199
  222.9 6.8 fusion.42
  229.8 9.5 fusion.52
  239.3 2.6 copy.102
  241.9 4.0 convert_element_type.126
  245.9 2.9 fusion.81
  249.5 26.6 %fusion.2 = (bf16[1280,2048]{1,0:T(8,128)(2,1)}, f32[1280,2048]{1,0:T(8,128)S(1)}) fusion(f32[2048]{0:T(1024)S(1)} %copy-done.61, bf16[512,2048]{1,0:T(8,128)(2,1)S(1)} %copy-done, f32[1280,512]{1,0:T(8,128)S(1)} %get-tuple-element.73, f32[512]{0:T(512)S(1)} %copy-done.48, f32[512]{0:T(512)S(1)} %copy-done.44, f32[1280]{0:T(1024)S(1)} %add_rsqrt_fusion, ...), kind=kOutput, calls=%fused_computation.5 | convolution fusion | flops 2860646400 | bytes 20469760 | tf_op jit(solution)/shard_map/dot_general | solution.py:102
  276.1 7.3 convert_reduce_fusion
  283.4 4.3 multiply_reduce_fusion.1
  293.2 5.6 reshape.276
  298.9 7.9 fusion.38
  309.6 4.9 fusion.40
  315.6 9.6 fusion.77
  325.2 12.3 %fusion.71 = f32[8,160,8]{2,1,0:T(8,128)S(1)} fusion(f32[8,160,8]{2,1,0:T(8,128)S(1)} %copy-done.21, f32[8,160,8,256]{3,2,1,0:T(8,128)} %get-tuple-element.68, f32[8,8,256]{2,1,0:T(8,128)S(1)} %copy-done.31, f32[8,160,8]{2,1,0:T(8,128)S(1)} %copy.107, f32[8,8,256,160]{2,3,1,0:T(8,128)S(1)} %fusion.77), kind=kLoop, calls=%fused_computation.153 | loop fusion | flops 18339840 | bytes 21159936 | tf_op jit(solution)/shard_map/reduce_sum | solution.py:42
  337.6 12.2 %fusion.25 = bf16[8,160,8,64]{3,2,1,0:T(8,128)(2,1)} fusion(bf16[8,160,8,64]{3,2,1,0:T(8,128)(2,1)S(1)} %copy-done.12, f32[8,160,8]{2,1,0:T(8,128)S(1)} %broadcast_multiply_fusion.2, bf16[64,256]{1,0:T(8,128)(2,1)S(1)} %copy-done.33, f32[8,8,256,160]{2,3,1,0:T(8,128)S(1)} %fusion.77, f32[8,160,8,256]{3,2,1,0:T(8,128)S(1)} %bitcast.130, ...), kind=kOutput, calls=%fused_computation.51 | convolution fusion | flops 359137280 | bytes 23814144 | tf_op jit(solution)/shard_map/cghm,dm->cghd/dot_general | solution.py:39
  349.9 4.5 reshape.294
  356.9 3.6 fusion.64
  360.8 124.3 %all-reduce.18.cloned.1.call-done = (f32[8,8,256,64]{2,3,1,0:T(8,128)}, f32[8,8,256]{2,1,0:T(8,128)}) async-done(((f32[8,8,256,64]{2,3,1,0:T(8,128)}, f32[8,8,256]{2,1,0:T(8,128)}), (f32[8,8,256,64]{2,3,1,0:T(8,128)}, f32[8,8,256]{2,1,0:T(8,128)})) %all-reduce.18.cloned.1.call-update) | async-done | bytes 4259856 | tf_op jit(solution)/shard_map/psum | solution.py:264
  485.1 6.5 fusion.82
  491.7 12.9 %fusion.54 = f32[8,160,8]{2,1,0:T(8,128)S(1)} fusion(f32[8,160,8]{2,1,0:T(8,128)} %copy-done.18, f32[8,160,8,256]{3,2,1,0:T(8,128)} %get-tuple-element.69, f32[8,8,256]{2,1,0:T(8,128)} %get-tuple-element.35, f32[8,8,256,160]{2,3,1,0:T(8,128)S(1)} %fusion.82), kind=kLoop, calls=%fused_computation.108 | loop fusion | flops 15718400 | bytes 21118976 | tf_op jit(solution)/shard_map/reduce_sum | solution.py:42
  504.8 13.3 %fusion.22 = bf16[8,160,8,64]{3,2,1,0:T(8,128)(2,1)} fusion(bf16[8,160,8,64]{3,2,1,0:T(8,128)(2,1)} %reshape.305, f32[8,160,8]{2,1,0:T(8,128)S(1)} %broadcast_multiply_fusion.1, f32[8,8,256,160]{2,3,1,0:T(8,128)} %copy-done.4, f32[8,160,8,256]{3,2,1,0:T(8,128)S(1)} %bitcast.128, f32[8,8,256]{2,1,0:T(8,128)S(1)} %copy-done.37, ...), kind=kOutput, calls=%fused_computation.48 | convolution fusion | flops 356515840 | bytes 23773184 | tf_op jit(solution)/shard_map/cghm,dm->cghd/dot_general | solution.py:39
  518.2 5.3 convert_bitcast_fusion
  524.9 3.2 reshape.279
  528.1 4.8 reshape.295
  535.3 5.9 multiply_reduce_fusion.2
  545.8 7.8 fusion.84
  554.3 8.4 fusion.75
  563.3 6.4 fusion.73
  574.1 5.6 broadcast_multiply_fusion
  579.7 3.2 reduce_sum.278
  582.9 107.7 %reduce-scatter.6.cloned.1.call-done = f32[48,512]{1,0:T(8,128)} async-done(((f32[768,512]{1,0:T(8,128)}), f32[48,512]{1,0:T(8,128)}) %reduce-scatter.6.cloned.1.call-update) | async-done | bytes 98320 | tf_op jit(solution)/shard_map/reduce_scatter | solution.py:321
  690.6 96.4 %reduce-scatter.14.cloned.1.call-done = f32[128,512]{1,0:T(8,128)} async-done(((f32[2048,512]{1,0:T(8,128)}), f32[128,512]{1,0:T(8,128)}) %reduce-scatter.14.cloned.1.call-update) | async-done | bytes 262160 | tf_op jit(solution)/shard_map/reduce_scatter | solution.py:333
  787.0 97.0 %reduce-scatter.12.cloned.1.call-done = f32[32,2048]{1,0:T(8,128)} async-done(((f32[512,2048]{1,0:T(8,128)}), f32[32,2048]{1,0:T(8,128)}) %reduce-scatter.12.cloned.1.call-update) | async-done | bytes 262160 | tf_op jit(solution)/shard_map/reduce_scatter | solution.py:331
  883.9 135.9 %reduce-scatter.8.cloned.1.call-done = f32[32,1536]{1,0:T(8,128)} async-done(((f32[512,1536]{1,0:T(8,128)}), f32[32,1536]{1,0:T(8,128)}) %reduce-scatter.8.cloned.1.call-update) | async-done | bytes 196624 | tf_op jit(solution)/shard_map/reduce_scatter | solution.py:325
  1019.9 7.9 fusion.47
  1028.5 75.0 %all-reduce.9 = (f32[512]{0:T(512)S(1)}, f32[512]{0:T(512)S(1)}, f32[512]{0:T(512)S(1)}, f32[1536]{0:T(1024)S(1)}, f32[512]{0:T(512)S(1)}, /*index=5*/f32[512]{0...) all-reduce(f32[512]{0:T(512)S(1)} %get-tuple-element.55, ...), channel_id=3, replica_groups=mesh['cell'=2,'gene'=16] {'gene'}, use_global_device_ids=true, to_apply=%region_26.27.clone | all-reduce | flops 7168 | bytes 57344
  1104.2 7.9 gather_fusion
  1112.1 3.0 all-reduce.12
  1115.1 3.9 fusion.48
  (232 shorter events, 50.1 us)
Async XLA Ops:
  7.2 242.2 %copy-start = (bf16[512,2048]{1,0:T(8,128)(2,1)S(1)}, bf16[512,2048]{1,0:T(8,128)(2,1)}, u32[]{:S(2)}) copy-start(bf16[512,2048]{1,0:T(8,128)(2,1)} %param.35) | copy-start | bytes 6291460
  7.2 8.4 copy-start.29
  7.2 8.4 copy-start.62
  7.2 215.7 %all-reduce.20.cloned.1.call-start = ((), (), s32[]{:S(2)}) async-start(), calls=%async_computation.11 | async-start | bytes 8519680 | tf_op jit(solution)/shard_map/psum | solution.py:199
  8.3 8.6 copy-start.38
  48.9 436.2 %all-reduce.18.cloned.1.call-start = ((), (), s32[]{:S(2)}) async-start(), calls=%async_computation.10 | async-start | bytes 8519680 | tf_op jit(solution)/shard_map/psum | solution.py:264
  248.8 38.8 %copy-start.3 = (f32[1280,512]{1,0:T(8,128)}, f32[1280,512]{1,0:T(8,128)S(1)}, u32[]{:S(2)}) copy-start(f32[1280,512]{1,0:T(8,128)S(1)} %get-tuple-element.73) | copy-start | bytes 7864324
  249.4 26.6 %copy-start.25 = (bf16[8,160,512]{2,1,0:T(8,128)(2,1)S(1)}, bf16[8,160,512]{2,1,0:T(8,128)(2,1)}, u32[]{:S(2)}) copy-start(bf16[8,160,512]{2,1,0:T(8,128)(2,1)} %param.39) | copy-start | bytes 3932164
  249.5 26.6 %copy-start.58 = (bf16[2048,512]{1,0:T(8,128)(2,1)S(1)}, bf16[2048,512]{1,0:T(8,128)(2,1)}, u32[]{:S(2)}) copy-start(bf16[2048,512]{1,0:T(8,128)(2,1)} %param.37) | copy-start | bytes 6291460
  315.1 10.1 copy-start.21
  315.1 10.1 copy-start.31
  315.2 267.8 %reduce-scatter.10.cloned.1.call-start = ((), (), s32[]{:S(2)}) async-start(), calls=%async_computation.7 | async-start | bytes 1114112 | tf_op jit(solution)/shard_map/reduce_scatter | solution.py:327
  315.6 22.0 %slice-start.5 = ((s8[10485760]{0:T(1024)(128)(4,1)}), s8[2097152]{0:T(1024)(128)(4,1)S(1)}, s32[]{:S(2)}) async-start(s8[10485760]{0:T(1024)(128)(4,1)} %bitcast.129), calls=%async_computation.18 | async-start | bytes 4194304
  315.6 22.0 %slice-start.6 = ((s8[10485760]{0:T(1024)(128)(4,1)}), s8[4194304]{0:T(1024)(128)(4,1)S(1)}, s32[]{:S(2)}) async-start(s8[10485760]{0:T(1024)(128)(4,1)} %bitcast.129), calls=%async_computation.19 | async-start | bytes 8388608
  325.2 12.4 %slice-start.7 = ((s8[10485760]{0:T(1024)(128)(4,1)}), s8[4194304]{0:T(1024)(128)(4,1)S(1)}, s32[]{:S(2)}) async-start(s8[10485760]{0:T(1024)(128)(4,1)} %bitcast.129), calls=%async_computation.20 | async-start | bytes 8388608
  325.2 12.4 %copy-start.12 = (bf16[8,160,8,64]{3,2,1,0:T(8,128)(2,1)S(1)}, bf16[8,160,8,64]{3,2,1,0:T(8,128)(2,1)}, u32[]{:S(2)}) copy-start(bf16[8,160,8,64]{3,2,1,0:T(8,128)(2,1)} %reshape.307) | copy-start | bytes 3932164
  325.2 12.4 %copy-start.33 = (bf16[64,256]{1,0:T(8,128)(2,1)S(1)}, bf16[64,256]{1,0:T(8,128)(2,1)}, u32[]{:S(2)}) copy-start(bf16[64,256]{1,0:T(8,128)(2,1)} %param.24) | copy-start | bytes 98308
  354.3 130.8 %copy-start.9 = (bf16[8,160,8,64]{1,3,2,0:T(8,128)(2,1)S(1)}, bf16[8,160,8,64]{1,3,2,0:T(8,128)(2,1)}, u32[]{:S(2)}) copy-start(bf16[8,160,8,64]{1,3,2,0:T(8,128)(2,1)} %copy.97) | copy-start | bytes 3932164
  360.6 330.0 %reduce-scatter.6.cloned.1.call-start = ((), (), s32[]{:S(2)}) async-start(), calls=%async_computation.5 | async-start | bytes 1671168 | tf_op jit(solution)/shard_map/reduce_scatter | solution.py:321
  485.1 19.6 %slice-start.2 = ((s8[10485760]{0:T(1024)(128)(4,1)}), s8[4194304]{0:T(1024)(128)(4,1)S(1)}, s32[]{:S(2)}) async-start(s8[10485760]{0:T(1024)(128)(4,1)} %bitcast.127), calls=%async_computation.15 | async-start | bytes 8388608
  485.1 19.6 %slice-start.3 = ((s8[10485760]{0:T(1024)(128)(4,1)}), s8[4194304]{0:T(1024)(128)(4,1)S(1)}, s32[]{:S(2)}) async-start(s8[10485760]{0:T(1024)(128)(4,1)} %bitcast.127), calls=%async_computation.16 | async-start | bytes 8388608
  491.7 13.0 %copy-start.4 = (f32[8,8,256,160]{2,3,1,0:T(8,128)}, f32[8,8,256,160]{2,3,1,0:T(8,128)S(1)}, u32[]{:S(2)}) copy-start(f32[8,8,256,160]{2,3,1,0:T(8,128)S(1)} %fusion.82) | copy-start | bytes 31457284
  491.7 13.1 %slice-start.4 = ((s8[10485760]{0:T(1024)(128)(4,1)}), s8[2097152]{0:T(1024)(128)(4,1)S(1)}, s32[]{:S(2)}) async-start(s8[10485760]{0:T(1024)(128)(4,1)} %bitcast.127), calls=%async_computation.17 | async-start | bytes 4194304
  491.7 13.1 %copy-start.19 = (f32[8,160,8]{2,1,0:T(8,128)S(1)}, f32[8,160,8]{2,1,0:T(8,128)}, u32[]{:S(2)}) copy-start(f32[8,160,8]{2,1,0:T(8,128)} %copy-done.18) | copy-start | bytes 122884
  491.7 13.1 %copy-start.34 = (bf16[64,256]{1,0:T(8,128)(2,1)S(1)}, bf16[64,256]{1,0:T(8,128)(2,1)}, u32[]{:S(2)}) copy-start(bf16[64,256]{1,0:T(8,128)(2,1)} %param.24) | copy-start | bytes 98308
  491.7 13.1 %copy-start.37 = (f32[8,8,256]{2,1,0:T(8,128)S(1)}, f32[8,8,256]{2,1,0:T(8,128)}, u32[]{:S(2)}) copy-start(f32[8,8,256]{2,1,0:T(8,128)} %get-tuple-element.35) | copy-start | bytes 196612
  491.7 26.4 %slice-start = ((s8[5242880]{0:T(1024)(128)(4,1)}), s8[4194304]{0:T(1024)(128)(4,1)S(1)}, s32[]{:S(2)}) async-start(s8[5242880]{0:T(1024)(128)(4,1)} %bitcast.125), calls=%async_computation.13 | async-start | bytes 8388608
  504.8 13.3 %slice-start.1 = ((s8[5242880]{0:T(1024)(128)(4,1)}), s8[1048576]{0:T(1024)(128)(4,1)S(1)}, s32[]{:S(2)}) async-start(s8[5242880]{0:T(1024)(128)(4,1)} %bitcast.125), calls=%async_computation.14 | async-start | bytes 2097152
  504.8 13.3 %copy-start.17 = (f32[8,8,256,64]{2,3,1,0:T(8,128)S(1)}, f32[8,8,256,64]{2,3,1,0:T(8,128)}, u32[]{:S(2)}) copy-start(f32[8,8,256,64]{2,3,1,0:T(8,128)} %get-tuple-element.34) | copy-start | bytes 12582916
  524.8 10.5 copy-start.22
  524.8 10.4 copy-start.36
  524.8 10.4 copy-start.43
  524.8 10.4 copy-start.57
  545.8 241.2 %reduce-scatter.14.cloned.1.call-start = ((), (), s32[]{:S(2)}) async-start(), calls=%async_computation.9 | async-start | bytes 4456448 | tf_op jit(solution)/shard_map/reduce_scatter | solution.py:333
  553.6 330.3 %reduce-scatter.12.cloned.1.call-start = ((), (), s32[]{:S(2)}) async-start(), calls=%async_computation.8 | async-start | bytes 4456448 | tf_op jit(solution)/shard_map/reduce_scatter | solution.py:331
  562.7 9.7 copy-start.47
  562.7 9.7 copy-start.39
  562.7 9.7 copy-start.46
  562.7 457.1 %reduce-scatter.8.cloned.1.call-start = ((), (), s32[]{:S(2)}) async-start(), calls=%async_computation.6 | async-start | bytes 3342336 | tf_op jit(solution)/shard_map/reduce_scatter | solution.py:325
  569.8 549.2 %all-reduce.22.cloned.1.call-start = ((), (), s32[]{:S(2)}) async-start(), calls=%async_computation.12 | async-start | bytes 2752512 | tf_op jit(solution)/shard_map/psum | solution.py:336
  579.7 440.1 %copy-start.65 = (f32[512]{0:T(512)S(1)}, f32[512]{0:T(512)}, u32[]{:S(2)}) copy-start(f32[512]{0:T(512)} %param.38) | copy-start | bytes 6148
  1019.9 8.0 copy-start.24
  1019.9 8.6 copy-start.50
  1019.9 8.6 copy-start.51
  1019.9 8.6 copy-start.54
  1019.9 8.6 copy-start.55
  1104.2 10.9 copy-start.52
  1115.1 13.7 %copy-start.1 = (bf16[512,2048]{1,0:T(8,128)(2,1)S(1)}, bf16[512,2048]{1,0:T(8,128)(2,1)}, u32[]{:S(2)}) copy-start(bf16[512,2048]{1,0:T(8,128)(2,1)} %param.35) | copy-start | bytes 6291460
  (37 other events, 147.1 us)
Sparse Core Ops, SparseCore 0:
  49.0 173.8 all-reduce.19
  315.3 169.8 all-reduce.17
  487.4 76.6 reduce-scatter.9
  569.4 121.1 reduce-scatter.5
  692.8 94.0 reduce-scatter.13
  789.2 94.6 reduce-scatter.11
  889.7 130.0 reduce-scatter.7
  1023.4 19.6 all-reduce.21
where the time goes:
time: 1150 us; the launch traced here: 1140 us
  waiting for transfers between devices  722 us (63%)
  matrix products  193 us (17%)
  blocking collectives  78 us (7%)
  local copies, waits for them, and re-layouts  73 us (6%)
  other arithmetic  51.7 us (4%)
  between operations  17.7 us (2%)
    psum x1, waiting for transfers between devices, local(): lax.psum((summary_in, total_in), 'gene')  160 us
    reduce_scatter x1, waiting for transfers between devices, local(): lax.psum_scatter(grad_joint_weight, 'gene', scatter_dimension=0, tiled=True)  136 us
    psum x1, waiting for transfers between devices, local(): lax.psum((local_grad_summary, local_grad_total), 'gene')  124 us
    reduce_scatter x1, waiting for transfers between devices, local(): lax.psum_scatter(grad_input_weight, 'gene', scatter_dimension=0, tiled=True)  108 us
    reduce_scatter x1, waiting for transfers between devices, local(): lax.psum_scatter(grad_upper_weight, 'gene', scatter_dimension=0, tiled=True)  97 us
    reduce_scatter x1, waiting for transfers between devices, local(): lax.psum_scatter(grad_lower_weight, 'gene', scatter_dimension=0, tiled=True)  96.4 us
    unnamed x1, blocking collectives  75 us
    dot_general x1, matrix products, forward_pass(): jnp.dot(normed_two_low, upper_weight, preferred_element_type=jnp.float32)  26.6 us
  transfers between devices with their start and end apart: 8, of which 6 were waited for; matrix products, arithmetic and copies ran while one was open for 15% of the time, Pallas kernels for 0%

commit v1 on v0

v1 whole, which is shorter than its diff:
```python
import jax
import jax.numpy as jnp
from jax import lax
from jax.experimental import pallas as pl
from jax.sharding import PartitionSpec as P

epsilon = 1e-05
highest = lax.Precision.HIGHEST


def normalize(values, gain_vector, shift_vector):
    centred = values - jnp.mean(values, axis=-1, keepdims=True)
    inverse = lax.rsqrt(jnp.mean(centred * centred, axis=-1, keepdims=True) + epsilon)
    scaled = centred * inverse
    return (scaled * gain_vector + shift_vector, scaled, inverse)


def normalize_back(grad_in, scaled, inverse, gain_vector):
    weighted = grad_in * gain_vector
    return inverse * (
        weighted
        - jnp.mean(weighted, axis=-1, keepdims=True)
        - scaled * jnp.mean(weighted * scaled, axis=-1, keepdims=True)
    )


def feature_map(heads_in, random_features, factor):
    projected = jnp.einsum(
        "cghd,dm->cghm", heads_in, random_features, preferred_element_type=jnp.float32
    )
    widened = heads_in.astype(jnp.float32)
    squared = jnp.sum(widened * widened, axis=-1, keepdims=True)
    feature_count = random_features.shape[1]
    return jnp.exp(factor * projected - 0.5 * factor * factor * squared) * feature_count ** (-0.5)


def feature_back(grad_feat, feature_values, heads_in, random_features, factor):
    weighted = grad_feat * feature_values
    projected_grad = (weighted * factor).astype(jnp.bfloat16)
    through = jnp.einsum(
        "cghm,dm->cghd", projected_grad, random_features, preferred_element_type=jnp.float32
    )
    return through - factor * factor * heads_in.astype(jnp.float32) * jnp.sum(
        weighted, axis=-1, keepdims=True
    )


def swap(value, axis, size, bit):
    return lax.ppermute(value, axis, [(i, i ^ bit) for i in range(size)])


def rounded(value):
    def kernel(wide_ref, low_ref):
        low_ref[...] = wide_ref[...].astype(jnp.bfloat16)

    return pl.pallas_call(
        kernel, out_shape=jax.ShapeDtypeStruct(value.shape, jnp.bfloat16), name="rounded"
    )(value)


def fence(value):
    return lax.optimization_barrier(value)


def sum_over_planes(mine_first, size, plane):
    high = [1 << b for b in range(size.bit_length()) if plane <= (1 << b) < size]
    mine = mine_first[0] + swap(mine_first[1], "gene", size, high[0])
    for bit in high[1:]:
        mine = mine + swap(mine, "gene", size, bit)
    return mine, swap(mine, "gene", size, high[0])


def local(
    encoder_packed_tokens,
    token_gene_index,
    cell_counts,
    zero_embed,
    random_features,
    input_weight,
    input_bias,
    first_gain,
    first_shift,
    joint_weight,
    joint_bias,
    output_weight,
    output_bias,
    second_gain,
    second_shift,
    upper_weight,
    upper_bias,
    lower_weight,
    lower_bias,
    cotangent,
):
    size = lax.axis_size("gene")
    plane = 4
    bf16 = jnp.bfloat16
    f32 = jnp.float32
    me = lax.axis_index("gene")
    core = lax.axis_index("cell")
    place = me % plane
    half_at = (me // plane) % 2
    cells_here, device_genes, width = cotangent.shape
    row_length = encoder_packed_tokens.shape[1]
    width_in = encoder_packed_tokens.shape[2]
    head_size, features = random_features.shape
    heads = width // head_size
    factor = head_size ** (-0.25)
    group = cells_here // plane
    first_gene = me * device_genes
    cell_ends = jnp.cumsum(cell_counts[0])
    slot_indices = jnp.arange(row_length, dtype=jnp.int32)
    segment = jnp.sum((slot_indices[:, None] >= cell_ends[None, :]).astype(jnp.int32), axis=1)
    living = segment < cells_here
    target_slot = jnp.where(living, segment * device_genes + token_gene_index[0] - first_gene, -1)
    places = jnp.arange(cells_here * device_genes, dtype=jnp.int32)
    select = target_slot[:, None] == places[None, :]
    scattered = jnp.einsum(
        "rt,ri->ti", select.astype(bf16), encoder_packed_tokens[0], preferred_element_type=f32
    )
    vacant = 1.0 - jnp.sum(select.astype(f32), axis=0)
    gene_rows = scattered + vacant[:, None] * jnp.tile(zero_embed.astype(f32), (cells_here, 1))
    gene_rows = gene_rows.astype(bf16)
    hidden_home = jnp.dot(gene_rows, input_weight, preferred_element_type=f32) + input_bias
    order = place ^ jnp.arange(plane)

    def out_and_in(home):
        parts = home.reshape(plane, group, device_genes, -1)[order]
        return jnp.stack([parts[0]] + [swap(parts[r], "gene", size, r) for r in range(1, plane)])

    def back_home(blocks):
        parts = jnp.stack(
            [blocks[0]] + [swap(blocks[r], "gene", size, r) for r in range(1, plane)]
        )
        return parts[order].reshape(cells_here, device_genes, -1)

    tokens = plane * group * device_genes
    cells_first = (1, 0, 2, 3)

    def by_cell(blocks):
        return blocks.transpose(cells_first).reshape(tokens, -1)

    def by_block(rows):
        return rows.reshape(group, plane, device_genes, -1).transpose(cells_first)

    hidden = by_cell(out_and_in(hidden_home))
    grad_out = fence(by_cell(out_and_in(cotangent.astype(f32))))
    grad_low = grad_out.astype(bf16)
    normed, scaled_one, inverse_one = normalize(hidden, first_gain, first_shift)
    normed_low = normed.astype(bf16)
    joint = (jnp.dot(normed_low, joint_weight, preferred_element_type=f32) + joint_bias).astype(bf16)
    per_cell = plane * device_genes
    split = (group, per_cell, heads, head_size)
    query = joint[:, :width].reshape(split)
    key_part = joint[:, width : 2 * width].reshape(split)
    value_part = joint[:, 2 * width :].reshape(split)
    query_low = feature_map(query, random_features, factor).astype(bf16)
    key_low = feature_map(key_part, random_features, factor).astype(bf16)

    def pack(summary, total):
        both = jnp.concatenate(
            [
                summary.reshape(group, 2, heads // 2 * head_size, features),
                jnp.pad(total.reshape(group, 2, heads // 2, features), ((0, 0), (0, 0), (0, 4), (0, 0))),
            ],
            axis=2,
        )
        return both[:, half_at ^ jnp.arange(2)]

    def unpack(pair):
        both = jnp.stack(pair)[half_at ^ jnp.arange(2)]
        rows = heads // 2 * head_size
        summary = both[:, :rows].reshape(heads, head_size, features)
        total = both[:, rows : rows + heads // 2].reshape(heads, features)
        return summary, total

    def over_genes(summary, total):
        packed = pack(summary, total)
        done = [unpack(sum_over_planes(packed[c], size, plane)) for c in range(group)]
        return jnp.stack([d[0] for d in done]), jnp.stack([d[1] for d in done])

    summary, total = over_genes(
        jnp.einsum("cghd,cghm->chdm", value_part, key_low, preferred_element_type=f32),
        jnp.sum(key_low, axis=1, dtype=f32),
    )
    summary_low = fence(summary).astype(bf16)
    total_low = fence(total).astype(bf16)
    numerator = jnp.einsum("cghm,chdm->cghd", query_low, summary_low, preferred_element_type=f32)
    denominator = jnp.einsum("cghm,chm->cgh", query_low, total_low, preferred_element_type=f32)
    attention = numerator / denominator[..., None]
    attention_low = attention.reshape(tokens, width).astype(bf16)
    middle = hidden + (
        jnp.dot(attention_low, output_weight, preferred_element_type=f32) + output_bias
    )
    normed_two, scaled_two, inverse_two = normalize(middle, second_gain, second_shift)
    normed_two_low = normed_two.astype(bf16)
    upper = jnp.dot(normed_two_low, upper_weight, preferred_element_type=f32) + upper_bias
    cumulative = 0.5 * (1.0 + lax.erf(upper * 0.7071067811865476))
    active_low = (upper * cumulative).astype(bf16)
    result = middle + jnp.dot(active_low, lower_weight, preferred_element_type=f32)
    block_out = (back_home(by_block(result)) + lower_bias).astype(bf16)
    grad_active = jnp.einsum("td,fd->tf", grad_low, lower_weight, preferred_element_type=f32)
    density = jnp.exp(-0.5 * upper * upper) * 0.3989422804014327
    upper_low = (grad_active * (cumulative + upper * density)).astype(bf16)
    grad_normed_two = jnp.einsum("tf,df->td", upper_low, upper_weight, preferred_element_type=f32)
    grad_middle = grad_out + normalize_back(grad_normed_two, scaled_two, inverse_two, second_gain)
    branch_low = grad_middle.astype(bf16)
    grad_attention = jnp.einsum(
        "td,ed->te", branch_low, output_weight, preferred_element_type=f32
    ).reshape(split)
    numerator_low = (grad_attention / denominator[..., None]).astype(bf16)
    grad_denominator = -jnp.sum(grad_attention * attention, axis=-1) / denominator
    grad_summary, grad_total = over_genes(
        jnp.einsum("cghd,cghm->chdm", numerator_low, query_low, preferred_element_type=f32),
        jnp.einsum("cghm,cgh->chm", query_low.astype(f32), grad_denominator, precision=highest),
    )
    grad_summary_low = fence(grad_summary).astype(bf16)
    grad_query_feat = (
        jnp.einsum("cghd,chdm->cghm", numerator_low, summary_low, preferred_element_type=f32)
        + grad_denominator[..., None] * total[:, None]
    )
    grad_key_feat = (
        jnp.einsum("cghd,chdm->cghm", value_part, grad_summary_low, preferred_element_type=f32)
        + grad_total[:, None]
    )
    grad_value = jnp.einsum(
        "cghm,chdm->cghd", key_low, grad_summary_low, preferred_element_type=f32
    )
    grad_query = feature_back(
        grad_query_feat, query_low.astype(f32), query, random_features, factor
    )
    grad_key = feature_back(grad_key_feat, key_low.astype(f32), key_part, random_features, factor)
    joint_low = jnp.concatenate(
        [
            grad_query.reshape(tokens, width),
            grad_key.reshape(tokens, width),
            grad_value.reshape(tokens, width),
        ],
        axis=1,
    ).astype(bf16)
    grad_normed = jnp.einsum("te,de->td", joint_low, joint_weight, preferred_element_type=f32)
    grad_hidden = grad_middle + normalize_back(grad_normed, scaled_one, inverse_one, first_gain)
    hidden_round = fence(grad_hidden.astype(bf16)).astype(f32)
    hidden_low = rounded(back_home(by_block(hidden_round)).reshape(cells_here * device_genes, width))

    def core_half(matrix):
        halves = jnp.stack(jnp.split(matrix, 2, axis=1))
        return halves[core] + swap(halves[1 - core], "cell", 2, 1)

    def shards(matrix):
        rows = matrix.shape[0] // size
        return matrix.reshape(size, rows * matrix.shape[1] // 256, 256)

    def scatter_sum(bundle, bits):
        rest = bundle[me ^ jnp.arange(size)]
        rest = rest.reshape((2,) * (size.bit_length() - 1) + rest.shape[1:])
        left = list(range(size.bit_length() - 2, -1, -1))
        for bit in bits:
            at = left.index(bit)
            left.pop(at)
            rest = lax.index_in_dim(rest, 0, at, keepdims=False) + swap(
                lax.index_in_dim(rest, 1, at, keepdims=False), "gene", size, 1 << bit
            )
        return rest

    grad_lower_weight = jnp.einsum("tf,td->fd", active_low, grad_low, preferred_element_type=f32)
    grad_upper_weight = jnp.einsum("td,tf->df", normed_two_low, upper_low, preferred_element_type=f32)
    grad_output_weight = jnp.einsum("te,td->ed", attention_low, branch_low, preferred_element_type=f32)
    grad_joint_weight = jnp.einsum("td,te->de", normed_low, joint_low, preferred_element_type=f32)
    grad_input_weight = jnp.einsum("ti,td->id", gene_rows, hidden_low, preferred_element_type=f32)
    small = [
        jnp.sum(hidden_low, axis=0, dtype=f32),
        jnp.sum(grad_normed * scaled_one, axis=0),
        jnp.sum(grad_normed, axis=0),
        jnp.sum(joint_low, axis=0, dtype=f32),
        jnp.sum(branch_low, axis=0, dtype=f32),
        jnp.sum(grad_normed_two * scaled_two, axis=0),
        jnp.sum(grad_normed_two, axis=0),
        jnp.sum(upper_low, axis=0, dtype=f32),
        jnp.sum(grad_out, axis=0),
    ]
    small_lengths = [v.shape[0] // size for v in small]
    vectors = jnp.concatenate([v.reshape(size, -1) for v in small], axis=1)
    vectors = vectors + swap(vectors, "cell", 2, 1)
    pad = (-vectors.shape[1]) % 256
    vectors = jnp.pad(vectors, ((0, 0), (0, pad))).reshape(size, -1, 256)
    log = size.bit_length() - 1
    mats_one = [grad_lower_weight, grad_upper_weight, grad_output_weight]
    mats_two = [grad_joint_weight, grad_input_weight]
    bundle_one = jnp.concatenate([shards(core_half(m)) for m in mats_one], axis=1)
    bundle_two = jnp.concatenate([shards(core_half(m)) for m in mats_two] + [vectors], axis=1)
    done_one = scatter_sum(bundle_one, list(range(log)))
    done_two = scatter_sum(bundle_two, list(range(log)))
    other_one = swap(done_one, "cell", 2, 1)
    other_two = swap(done_two, "cell", 2, 1)

    def open_bundle(mine, other, mats):
        first = jnp.where(core == 0, mine, other)
        second = jnp.where(core == 0, other, mine)
        out = []
        at = 0
        for m in mats:
            rows = m.shape[0] // size
            count = rows * m.shape[1] // 2 // 256
            out.append(
                jnp.concatenate(
                    [b[at : at + count].reshape(rows, m.shape[1] // 2) for b in (first, second)],
                    axis=1,
                )
            )
            at += count
        return out, at

    (g_lower, g_upper, g_output), at = open_bundle(done_one, other_one, mats_one)
    (g_joint, g_input), at = open_bundle(done_two, other_two, mats_two)
    flat = done_two[at:].reshape(-1)
    small_out = []
    at = 0
    for length in small_lengths:
        small_out.append(flat[at : at + length])
        at += length
    picked = jnp.einsum("rt,td->rd", select.astype(bf16), hidden_low, preferred_element_type=f32)
    token_grad = jnp.einsum(
        "rd,id->ri", picked.astype(bf16), input_weight, preferred_element_type=f32
    ).reshape(1, row_length, width_in)
    zero_hidden = jnp.sum(
        (vacant[:, None] * hidden_low.astype(f32)).reshape(cells_here, device_genes, width), axis=0
    )
    zero_hidden = zero_hidden + swap(zero_hidden, "cell", 2, 1)
    zero_grad = jnp.einsum("td,id->ti", zero_hidden, input_weight.astype(f32), precision=highest)
    return (
        block_out,
        token_grad,
        zero_grad,
        g_input,
        small_out[0],
        small_out[1],
        small_out[2],
        g_joint,
        small_out[3],
        g_output,
        small_out[4],
        small_out[5],
        small_out[6],
        g_upper,
        small_out[7],
        g_lower,
        small_out[8],
    )


def solution(mesh):
    return jax.shard_map(
        local,
        mesh=mesh,
        in_specs=(
            P("cell", "gene", None),
            P("cell", "gene"),
            P("cell", "gene"),
            P("gene", None),
            P(),
            P(),
            P(),
            P(),
            P(),
            P(),
            P(),
            P(),
            P(),
            P(),
            P(),
            P(),
            P(),
            P(),
            P(),
            P("cell", "gene", None),
        ),
        out_specs=(
            P("cell", "gene", None),
            P("cell", "gene", None),
            P("gene", None),
            P("gene", None),
            P("gene"),
            P("gene"),
            P("gene"),
            P("gene", None),
            P("gene"),
            P("gene", None),
            P("gene"),
            P("gene"),
            P("gene"),
            P("gene", None),
            P("gene"),
            P("gene", None),
            P("gene"),
        ),
        check_vma=False,
    )
```

time: 1150 us -> 590 us (0.51)
  waiting for transfers between devices: 722 us -> 231 us
  matrix products: 193 us -> 108 us
  blocking collectives: 78 us -> 0 us
  local copies, waits for them, and re-layouts: 73 us -> 113 us
  starting transfers between devices: 1.63 us -> 39.2 us
  other arithmetic: 51.7 us -> 85 us
  between operations: 17.7 us -> 2.66 us
    reduce_scatter x5 -> x0, waiting for transfers between devices: 437 us -> none  [the longest x1 136 us: local(): lax.psum_scatter(grad_joint_weight, 'gene', scatter_dimension=0, tiled=True)]
    psum x3 -> x0, waiting for transfers between devices: 284 us -> none  [the longest x1 160 us: local(): lax.psum((summary_in, total_in), 'gene')]
    ppermute x0 -> x41, waiting for transfers between devices: none -> 231 us  [swap(): return lax.ppermute(value, axis, [(i, i ^ bit) for i in range(size)])]
    unnamed x1 -> x0, blocking collectives: 75 us -> none
    dot_general x21 -> x22, matrix products: 139 us -> 82.6 us  [the longest x1 7.79 us: local(): jnp.einsum('td,fd->tf', grad_low, lower_weight, preferred_element_type=f32)]
    ppermute x0 -> x41, starting transfers between devices: none -> 39.2 us  [swap(): return lax.ppermute(value, axis, [(i, i ^ bit) for i in range(size)])]
    gather x1 -> x12, local copies, waits for them, and re-layouts: 7.87 us -> 32.5 us  [the longest x2 9.46 us: scatter_sum(): rest = bundle[me ^ jnp.arange(size)]]
    reduce_sum x8 -> x6, other arithmetic: 34 us -> 9.43 us  [the longest x1 3.36 us: local(): jnp.sum(hidden_low, axis=0, dtype=f32)]
  transfers between devices with their start and end apart: 8 -> 41, of which waited for: 6 -> 24; matrix products, arithmetic and copies ran while one was open for 15% -> 31% of each run, Pallas kernels for 0% -> 1%
where the time goes in v1:
time: 590 us; the launch traced here: 581 us
  waiting for transfers between devices  231 us (39%)
  local copies, waits for them, and re-layouts  113 us (19%)
  matrix products  108 us (18%)
  other arithmetic  85 us (14%)
  starting transfers between devices  39.2 us (7%)
    ppermute x41, waiting for transfers between devices, swap(): return lax.ppermute(value, axis, [(i, i ^ bit) for i in range(size)])  231 us
    ppermute x41, starting transfers between devices, swap(): return lax.ppermute(value, axis, [(i, i ^ bit) for i in range(size)])  39.2 us
    add x5, other arithmetic, core_half(): return halves[core] + swap(halves[1 - core], 'cell', 2, 1)  14.7 us
    unnamed x159, local copies, waits for them, and re-layouts  12 us
  transfers between devices with their start and end apart: 41, of which 24 were waited for; matrix products, arithmetic and copies ran while one was open for 31% of the time, Pallas kernels for 1%

profile of v1, /device:TPU:0, one launch (start us, length us, event | category | flops | bytes accessed | tf_op | source)
XLA Modules:
  0.0 581.4 jit_solution(11896460620676245352)
XLA Ops:
  4.1 4.5 fusion.17
  11.3 3.9 gather_fusion
  24.7 3.9 gather_fusion.5
  28.6 7.7 %collective-permute-done.1 = f32[2,160,512]{2,1,0:T(8,128)S(1)} collective-permute-done((f32[2,160,512]{2,1,0:T(8,128)}, f32[2,160,512]{2,1,0:T(8,128)S(1)}, u32[]{:S(2)}, u32[]{:S(2)}) %collective-permute-start.1) | collective-permute-done | bytes 655392 | tf_op jit(solution)/shard_map/ppermute | solution.py:49
  39.3 12.3 %collective-permute-done.2 = f32[2,160,512]{2,1,0:T(8,128)} collective-permute-done((f32[2,160,512]{2,1,0:T(8,128)}, f32[2,160,512]{2,1,0:T(8,128)}, u32[]{:S(2)}, u32[]{:S(2)}) %collective-permute-start.2) | collective-permute-done | bytes 655392 | tf_op jit(solution)/shard_map/ppermute | solution.py:49
  66.1 4.7 reshape.507
  70.8 4.1 copy.194
  77.4 3.4 copy.192
  81.2 4.8 convert_reduce_fusion
  86.0 3.9 fusion.110
  95.9 3.5 slice_bitcast_fusion.21
  114.5 16.1 %collective-permute-done.7 = f32[264,256]{1,0:T(8,128)S(1)} collective-permute-done((f32[264,256]{1,0:T(8,128)S(1)}, f32[264,256]{1,0:T(8,128)S(1)}, u32[]{:S(2)}, u32[]{:S(2)}) %collective-permute-start.7) | collective-permute-done | bytes 270368 | tf_op jit(solution)/shard_map/ppermute | solution.py:49
  130.6 4.6 multiply_convert_fusion.3
  142.6 4.4 collective-permute-done.5
  149.7 4.1 fusion.86
  153.8 5.7 fusion.108
  163.1 3.8 multiply_convert_fusion.2
  167.0 7.8 %convert_reduce_fusion.1 = (f32[2048]{0:T(1024)S(1)}, bf16[1280,2048]{1,0:T(8,128)(2,1)S(1)}) fusion(f32[1280,2048]{1,0:T(8,128)S(1)} %get-tuple-element.89, f32[2048]{0:T(1024)S(1)} %copy-done.63, bf16[2048,512]{1,0:T(8,128)(2,1)S(1)} %copy-done.58, f32[1280,512]{1,0:T(8,128)S(1)} %bitcast.397), kind=kOutput, calls=%fused_computation.23 | convolution fusion | flops 2719086592 | bytes 20463616 | tf_op jit(solution)/shard_map/td,fd->tf/dot_general | solution.py:202
  174.8 3.8 multiply_reduce_fusion
  198.1 4.7 reshape.372
  202.8 5.3 fusion.99
  209.5 6.2 %fusion.9 = (f32[2,640,8]{1,2,0:T(8,128)S(1)}, f32[2,8,256,640]{2,3,1,0:T(8,128)}) fusion(bf16[2,640,8,256]{3,1,2,0:T(8,128)(2,1)S(1)} %bitcast.388, f32[2,8,256]{2,1,0:T(8,128)S(1)} %constant_dynamic-update-slice_fusion, f32[2,640,8]{1,2,0:T(8,128)S(1)} %negate_divide_fusion, bf16[2,8,64,256]{3,2,1,0:T(8,128)(2,1)S(1)} %copy-done.45, ...), kind=kOutput, calls=%fused_computation.34 | convolution fusion | flops 349952000 | bytes 19013632 | tf_op jit(solution)/shard_map/cghd,chdm->cghm/dot_general | solution.py:219
  226.5 3.7 fusion.31
  230.3 3.6 collective-permute-done.15
  233.8 4.9 collective-permute-done.18
  241.1 5.7 fusion.24
  249.1 10.7 %collective-permute-done.16 = f32[264,256]{1,0:T(8,128)S(1)} collective-permute-done((f32[264,256]{1,0:T(8,128)S(1)}, f32[264,256]{1,0:T(8,128)S(1)}, u32[]{:S(2)}, u32[]{:S(2)}) %collective-permute-start.16) | collective-permute-done | bytes 270368 | tf_op jit(solution)/shard_map/ppermute | solution.py:49
  261.2 3.7 collective-permute-done.19
  272.0 4.4 collective-permute-done.20
  279.9 4.5 fusion.47
  294.6 4.1 fusion.111
  298.7 3.4 multiply_reduce_fusion.1
  313.9 8.9 %collective-permute-done.21 = f32[2,160,512]{2,1,0:T(8,128)} collective-permute-done((f32[2,160,512]{2,1,0:T(8,128)}, f32[2,160,512]{2,1,0:T(8,128)}, u32[]{:S(2)}, u32[]{:S(2)}) %collective-permute-start.21) | collective-permute-done | bytes 655392 | tf_op jit(solution)/shard_map/ppermute | solution.py:49
  322.8 14.1 %collective-permute-done.23 = f32[2,160,512]{2,1,0:T(8,128)} collective-permute-done((f32[2,160,512]{2,1,0:T(8,128)}, f32[2,160,512]{2,1,0:T(8,128)}, u32[]{:S(2)}, u32[]{:S(2)}) %collective-permute-start.23) | collective-permute-done | bytes 655392 | tf_op jit(solution)/shard_map/ppermute | solution.py:49
  341.4 4.0 gather_fusion.9
  356.9 4.5 fusion.34
  370.1 5.5 gather_fusion.11
  384.5 4.0 gather_fusion.10
  396.1 4.8 convolution_add_fusion.3
  405.8 14.0 %collective-permute-done.28 = f32[2,2,2,146,256]{4,2,3,1,0:T(2,128)S(1)} collective-permute-done((f32[2,2,2,146,256]{4,2,3,1,0:T(2,128)S(1)}, f32[2,2,2,146,256]{4,2,3,1,0:T(2,128)S(1)}, u32[]{:S(2)}, u32[]{:S(2)}) %collective-permute-start.28) | collective-permute-done | bytes 1196064 | tf_op jit(solution)/shard_map/ppermute | solution.py:49
  421.7 62.7 %collective-permute-done.9 = f32[2,160,512]{2,1,0:T(8,128)S(1)} collective-permute-done((f32[2,160,512]{2,1,0:T(8,128)}, f32[2,160,512]{2,1,0:T(8,128)S(1)}, u32[]{:S(2)}, u32[]{:S(2)}) %collective-permute-start.9) | collective-permute-done | bytes 655392 | tf_op jit(solution)/shard_map/ppermute | solution.py:49
  484.4 12.1 %collective-permute-done.11 = f32[2,160,512]{2,1,0:T(8,128)} collective-permute-done((f32[2,160,512]{2,1,0:T(8,128)}, f32[2,160,512]{2,1,0:T(8,128)}, u32[]{:S(2)}, u32[]{:S(2)}) %collective-permute-start.11) | collective-permute-done | bytes 655392 | tf_op jit(solution)/shard_map/ppermute | solution.py:49
  499.7 4.1 gather_fusion.4
  517.7 4.0 convolution_bitcast_fusion
  521.7 5.8 collective-permute-done.30
  530.8 13.3 %collective-permute-done.37 = f32[2,2,288,256]{3,2,1,0:T(8,128)} collective-permute-done((f32[2,2,288,256]{3,2,1,0:T(8,128)}, f32[2,2,288,256]{3,2,1,0:T(8,128)}, u32[]{:S(2)}, u32[]{:S(2)}) %collective-permute-start.37) | collective-permute-done | bytes 1179680 | tf_op jit(solution)/shard_map/ppermute | solution.py:49
  547.9 13.1 %collective-permute-done.38 = f32[2,288,256]{2,1,0:T(8,128)S(1)} collective-permute-done((f32[2,288,256]{2,1,0:T(8,128)S(1)}, f32[2,288,256]{2,1,0:T(8,128)S(1)}, u32[]{:S(2)}, u32[]{:S(2)}) %collective-permute-start.38) | collective-permute-done | bytes 589856 | tf_op jit(solution)/shard_map/ppermute | solution.py:49
  565.9 11.0 %collective-permute-done.39 = f32[288,256]{1,0:T(8,128)S(1)} collective-permute-done((f32[288,256]{1,0:T(8,128)}, f32[288,256]{1,0:T(8,128)S(1)}, u32[]{:S(2)}, u32[]{:S(2)}) %collective-permute-start.39) | collective-permute-done | bytes 294944 | tf_op jit(solution)/shard_map/ppermute | solution.py:49
  (406 shorter events, 220.8 us)
Async XLA Ops:
  0.7 162.2 %copy-start = (bf16[512,2048]{1,0:T(8,128)(2,1)S(1)}, bf16[512,2048]{1,0:T(8,128)(2,1)}, u32[]{:S(2)}) copy-start(bf16[512,2048]{1,0:T(8,128)(2,1)} %param.35) | copy-start | bytes 6291460
  4.1 20.6 %copy-start.50 = (s32[1024]{0:T(1024)}, s32[1024]{0:T(1024)S(1)}, u32[]{:S(2)}) copy-start(s32[1024]{0:T(1024)S(1)} %get-tuple-element.99) | copy-start | bytes 12292
  18.4 17.9 %collective-permute-start.1 = (f32[2,160,512]{2,1,0:T(8,128)}, f32[2,160,512]{2,1,0:T(8,128)S(1)}, u32[]{:S(2)}, u32[]{:S(2)}) collective-permute-start(f32[2,160,512]{2,1,0:T(8,128)} %get-tuple-element.50), channel_id=1, source_target_pairs={{0,2},{1,3},{2,0},{3,1},{4,6},{5,7},{6,4},{7,5},{8,10},{9,11},{10,... | collective-permute-start | bytes 1966088 | tf_op jit(solution)/shard_map/ppermute | solution.py:49
  21.3 18.0 %collective-permute-start = (f32[2,160,512]{2,1,0:T(8,128)}, f32[2,160,512]{2,1,0:T(8,128)}, u32[]{:S(2)}, u32[]{:S(2)}) collective-permute-start(f32[2,160,512]{2,1,0:T(8,128)} %get-tuple-element.51), channel_id=1, source_target_pairs={{0,1},{1,0},{2,3},{3,2},{4,5},{5,4},{6,7},{7,6},{8,9},{9,8},{10,11... | collective-permute-start | bytes 1966088 | tf_op jit(solution)/shard_map/ppermute | solution.py:49
  22.8 28.8 %collective-permute-start.2 = (f32[2,160,512]{2,1,0:T(8,128)}, f32[2,160,512]{2,1,0:T(8,128)}, u32[]{:S(2)}, u32[]{:S(2)}) collective-permute-start(f32[2,160,512]{2,1,0:T(8,128)} %get-tuple-element.52), channel_id=1, source_target_pairs={{0,3},{1,2},{2,1},{3,0},{4,7},{5,6},{6,5},{7,4},{8,11},{9,10},{10,... | collective-permute-start | bytes 1966088 | tf_op jit(solution)/shard_map/ppermute | solution.py:49
  93.8 15.5 %collective-permute-start.6 = (f32[264,256]{1,0:T(8,128)}, f32[264,256]{1,0:T(8,128)}, u32[]{:S(2)}, u32[]{:S(2)}) collective-permute-start(f32[264,256]{1,0:T(8,128)} %get-tuple-element.63), channel_id=1, source_target_pairs={{0,4},{1,5},{2,6},{3,7},{4,0},{5,1},{6,2},{7,3},{8,12},{9,13},{10,... | collective-permute-start | bytes 811016 | tf_op jit(solution)/shard_map/ppermute | solution.py:49
  95.6 13.7 %collective-permute-start.3 = (f32[264,256]{1,0:T(8,128)}, f32[264,256]{1,0:T(8,128)}, u32[]{:S(2)}, u32[]{:S(2)}) collective-permute-start(f32[264,256]{1,0:T(8,128)} %get-tuple-element.64), channel_id=1, source_target_pairs={{0,4},{1,5},{2,6},{3,7},{4,0},{5,1},{6,2},{7,3},{8,12},{9,13},{10,... | collective-permute-start | bytes 811016 | tf_op jit(solution)/shard_map/ppermute | solution.py:49
  99.4 38.0 %collective-permute-start.13 = (f32[2,160,512]{2,1,0:T(8,128)}, f32[2,160,512]{2,1,0:T(8,128)}, u32[]{:S(2)}, u32[]{:S(2)}) collective-permute-start(f32[2,160,512]{2,1,0:T(8,128)} %get-tuple-element.42), channel_id=1, source_target_pairs={{0,2},{1,3},{2,0},{3,1},{4,6},{5,7},{6,4},{7,5},{8,10},{9,11},{10,... | collective-permute-start | bytes 1966088 | tf_op jit(solution)/shard_map/ppermute | solution.py:49
  101.0 36.4 %collective-permute-start.12 = (f32[2,160,512]{2,1,0:T(8,128)}, f32[2,160,512]{2,1,0:T(8,128)}, u32[]{:S(2)}, u32[]{:S(2)}) collective-permute-start(f32[2,160,512]{2,1,0:T(8,128)} %get-tuple-element.43), channel_id=1, source_target_pairs={{0,1},{1,0},{2,3},{3,2},{4,5},{5,4},{6,7},{7,6},{8,9},{9,8},{10,11... | collective-permute-start | bytes 1966088 | tf_op jit(solution)/shard_map/ppermute | solution.py:49
  102.5 34.9 %collective-permute-start.14 = (f32[2,160,512]{2,1,0:T(8,128)}, f32[2,160,512]{2,1,0:T(8,128)}, u32[]{:S(2)}, u32[]{:S(2)}) collective-permute-start(f32[2,160,512]{2,1,0:T(8,128)} %get-tuple-element.44), channel_id=1, source_target_pairs={{0,3},{1,2},{2,1},{3,0},{4,7},{5,6},{6,5},{7,4},{8,11},{9,10},{10,... | collective-permute-start | bytes 1966088 | tf_op jit(solution)/shard_map/ppermute | solution.py:49
  109.3 26.0 %copy-start.15 = (bf16[2,640,8,64]{1,3,2,0:T(8,128)(2,1)}, bf16[2,640,8,64]{1,3,2,0:T(8,128)(2,1)S(1)}, u32[]{:S(2)}) copy-start(bf16[2,640,8,64]{1,3,2,0:T(8,128)(2,1)S(1)} %copy.198) | copy-start | bytes 3932164
  111.1 19.5 %collective-permute-start.7 = (f32[264,256]{1,0:T(8,128)S(1)}, f32[264,256]{1,0:T(8,128)S(1)}, u32[]{:S(2)}, u32[]{:S(2)}) collective-permute-start(f32[264,256]{1,0:T(8,128)S(1)} %get-tuple-element.61), channel_id=1, source_target_pairs={{0,8},{1,9},{2,10},{3,11},{4,12},{5,13},{6,14},{7,15},{8,0},{9,1},... | collective-permute-start | bytes 811016 | tf_op jit(solution)/shard_map/ppermute | solution.py:49
  114.1 21.3 %collective-permute-start.4 = (f32[264,256]{1,0:T(8,128)S(1)}, f32[264,256]{1,0:T(8,128)S(1)}, u32[]{:S(2)}, u32[]{:S(2)}) collective-permute-start(f32[264,256]{1,0:T(8,128)S(1)} %get-tuple-element.62), channel_id=1, source_target_pairs={{0,8},{1,9},{2,10},{3,11},{4,12},{5,13},{6,14},{7,15},{8,0},{9,1},... | collective-permute-start | bytes 811016 | tf_op jit(solution)/shard_map/ppermute | solution.py:49
  130.6 10.7 %collective-permute-start.8 = (f32[264,256]{1,0:T(8,128)S(1)}, f32[264,256]{1,0:T(8,128)S(1)}, u32[]{:S(2)}, u32[]{:S(2)}) collective-permute-start(f32[264,256]{1,0:T(8,128)S(1)} %add.271), channel_id=1, source_target_pairs={{0,4},{1,5},{2,6},{3,7},{4,0},{5,1},{6,2},{7,3},{8,12},{9,13},{10,... | collective-permute-start | bytes 811016 | tf_op jit(solution)/shard_map/ppermute | solution.py:49
  135.5 11.6 %collective-permute-start.5 = (f32[264,256]{1,0:T(8,128)S(1)}, f32[264,256]{1,0:T(8,128)}, u32[]{:S(2)}, u32[]{:S(2)}) collective-permute-start(f32[264,256]{1,0:T(8,128)S(1)} %add.269), channel_id=1, source_target_pairs={{0,4},{1,5},{2,6},{3,7},{4,0},{5,1},{6,2},{7,3},{8,12},{9,13},{10,... | collective-permute-start | bytes 811016 | tf_op jit(solution)/shard_map/ppermute | solution.py:49
  162.3 19.6 %copy-start.2 = (f32[1280,512]{1,0:T(8,128)}, f32[1280,512]{1,0:T(8,128)S(1)}, u32[]{:S(2)}) copy-start(f32[1280,512]{1,0:T(8,128)S(1)} %get-tuple-element.87) | copy-start | bytes 7864324
  167.0 20.4 %copy-start.67 = (bf16[1280,2048]{1,0:T(8,128)(2,1)}, bf16[1280,2048]{1,0:T(8,128)(2,1)S(1)}, u32[]{:S(2)}) copy-start(bf16[1280,2048]{1,0:T(8,128)(2,1)S(1)} %get-tuple-element.88) | copy-start | bytes 15728644
  192.8 171.7 %collective-permute-start.33 = (f32[2048,256]{1,0:T(8,128)}, f32[2048,256]{1,0:T(8,128)}, u32[]{:S(2)}, u32[]{:S(2)}) collective-permute-start(f32[2048,256]{1,0:T(8,128)} %fusion.36), channel_id=1, source_target_pairs={{0,16},{16,0},{1,17},{17,1},{2,18},{18,2},{3,19},{19,3},{4,20},{20... | collective-permute-start | bytes 6291464 | tf_op jit(solution)/shard_map/ppermute | solution.py:49
  197.6 67.9 %collective-permute-start.35 = (f32[512,256]{1,0:T(8,128)}, f32[512,256]{1,0:T(8,128)}, u32[]{:S(2)}, u32[]{:S(2)}) collective-permute-start(f32[512,256]{1,0:T(8,128)} %fusion.61), channel_id=1, source_target_pairs={{0,16},{16,0},{1,17},{17,1},{2,18},{18,2},{3,19},{19,3},{4,20},{20... | collective-permute-start | bytes 1572872 | tf_op jit(solution)/shard_map/ppermute | solution.py:49
  220.3 20.8 %slice-start.4 = ((s8[5242880]{0:T(1024)(128)(4,1)}), s8[1048576]{0:T(1024)(128)(4,1)S(1)}, s32[]{:S(2)}) async-start(s8[5242880]{0:T(1024)(128)(4,1)} %bitcast.389), calls=%async_computation.4 | async-start | bytes 2097152
  224.4 9.4 %collective-permute-start.15 = (f32[264,256]{1,0:T(8,128)S(1)}, f32[264,256]{1,0:T(8,128)S(1)}, u32[]{:S(2)}, u32[]{:S(2)}) collective-permute-start(f32[264,256]{1,0:T(8,128)S(1)} %get-tuple-element.59), channel_id=1, source_target_pairs={{0,4},{1,5},{2,6},{3,7},{4,0},{5,1},{6,2},{7,3},{8,12},{9,13},{10,... | collective-permute-start | bytes 811016 | tf_op jit(solution)/shard_map/ppermute | solution.py:49
  224.5 14.2 %collective-permute-start.18 = (f32[264,256]{1,0:T(8,128)S(1)}, f32[264,256]{1,0:T(8,128)S(1)}, u32[]{:S(2)}, u32[]{:S(2)}) collective-permute-start(f32[264,256]{1,0:T(8,128)S(1)} %get-tuple-element.60), channel_id=1, source_target_pairs={{0,4},{1,5},{2,6},{3,7},{4,0},{5,1},{6,2},{7,3},{8,12},{9,13},{10,... | collective-permute-start | bytes 811016 | tf_op jit(solution)/shard_map/ppermute | solution.py:49
  230.3 126.7 %collective-permute-start.34 = (f32[512,1024]{1,0:T(8,128)}, f32[512,1024]{1,0:T(8,128)}, u32[]{:S(2)}, u32[]{:S(2)}) collective-permute-start(f32[512,1024]{1,0:T(8,128)} %fusion.31), channel_id=1, source_target_pairs={{0,16},{16,0},{1,17},{17,1},{2,18},{18,2},{3,19},{19,3},{4,20},{20... | collective-permute-start | bytes 6291464 | tf_op jit(solution)/shard_map/ppermute | solution.py:49
  238.8 21.1 %collective-permute-start.16 = (f32[264,256]{1,0:T(8,128)S(1)}, f32[264,256]{1,0:T(8,128)S(1)}, u32[]{:S(2)}, u32[]{:S(2)}) collective-permute-start(f32[264,256]{1,0:T(8,128)S(1)} %get-tuple-element.57), channel_id=1, source_target_pairs={{0,8},{1,9},{2,10},{3,11},{4,12},{5,13},{6,14},{7,15},{8,0},{9,1},... | collective-permute-start | bytes 811016 | tf_op jit(solution)/shard_map/ppermute | solution.py:49
  248.4 16.5 %collective-permute-start.19 = (f32[264,256]{1,0:T(8,128)S(1)}, f32[264,256]{1,0:T(8,128)S(1)}, u32[]{:S(2)}, u32[]{:S(2)}) collective-permute-start(f32[264,256]{1,0:T(8,128)S(1)} %get-tuple-element.58), channel_id=1, source_target_pairs={{0,8},{1,9},{2,10},{3,11},{4,12},{5,13},{6,14},{7,15},{8,0},{9,1},... | collective-permute-start | bytes 811016 | tf_op jit(solution)/shard_map/ppermute | solution.py:49
  259.9 10.7 %collective-permute-start.17 = (f32[264,256]{1,0:T(8,128)S(1)}, f32[264,256]{1,0:T(8,128)S(1)}, u32[]{:S(2)}, u32[]{:S(2)}) collective-permute-start(f32[264,256]{1,0:T(8,128)S(1)} %add.289), channel_id=1, source_target_pairs={{0,4},{1,5},{2,6},{3,7},{4,0},{5,1},{6,2},{7,3},{8,12},{9,13},{10,... | collective-permute-start | bytes 811016 | tf_op jit(solution)/shard_map/ppermute | solution.py:49
  264.9 11.5 %collective-permute-start.20 = (f32[264,256]{1,0:T(8,128)S(1)}, f32[264,256]{1,0:T(8,128)}, u32[]{:S(2)}, u32[]{:S(2)}) collective-permute-start(f32[264,256]{1,0:T(8,128)S(1)} %add.291), channel_id=1, source_target_pairs={{0,4},{1,5},{2,6},{3,7},{4,0},{5,1},{6,2},{7,3},{8,12},{9,13},{10,... | collective-permute-start | bytes 811016 | tf_op jit(solution)/shard_map/ppermute | solution.py:49
  304.9 17.9 %collective-permute-start.21 = (f32[2,160,512]{2,1,0:T(8,128)}, f32[2,160,512]{2,1,0:T(8,128)}, u32[]{:S(2)}, u32[]{:S(2)}) collective-permute-start(f32[2,160,512]{2,1,0:T(8,128)} %get-tuple-element.38), channel_id=1, source_target_pairs={{0,1},{1,0},{2,3},{3,2},{4,5},{5,4},{6,7},{7,6},{8,9},{9,8},{10,11... | collective-permute-start | bytes 1966088 | tf_op jit(solution)/shard_map/ppermute | solution.py:49
  306.4 30.6 %collective-permute-start.23 = (f32[2,160,512]{2,1,0:T(8,128)}, f32[2,160,512]{2,1,0:T(8,128)}, u32[]{:S(2)}, u32[]{:S(2)}) collective-permute-start(f32[2,160,512]{2,1,0:T(8,128)} %get-tuple-element.39), channel_id=1, source_target_pairs={{0,3},{1,2},{2,1},{3,0},{4,7},{5,6},{6,5},{7,4},{8,11},{9,10},{10,... | collective-permute-start | bytes 1966088 | tf_op jit(solution)/shard_map/ppermute | solution.py:49
  307.9 30.2 %collective-permute-start.22 = (f32[2,160,512]{2,1,0:T(8,128)S(1)}, f32[2,160,512]{2,1,0:T(8,128)}, u32[]{:S(2)}, u32[]{:S(2)}) collective-permute-start(f32[2,160,512]{2,1,0:T(8,128)S(1)} %get-tuple-element.40), channel_id=1, source_target_pairs={{0,2},{1,3},{2,0},{3,1},{4,6},{5,7},{6,4},{7,5},{8,10},{9,11},{10,... | collective-permute-start | bytes 1966088 | tf_op jit(solution)/shard_map/ppermute | solution.py:49
  322.8 55.3 %collective-permute-start.25 = (f32[512,768]{1,0:T(8,128)}, f32[512,768]{1,0:T(8,128)}, u32[]{:S(2)}, u32[]{:S(2)}) collective-permute-start(f32[512,768]{1,0:T(8,128)} %fusion.41), channel_id=1, source_target_pairs={{0,16},{16,0},{1,17},{17,1},{2,18},{18,2},{3,19},{19,3},{4,20},{20... | collective-permute-start | bytes 4718600 | tf_op jit(solution)/shard_map/ppermute | solution.py:49
  354.1 2.7 collective-permute-start.27
  355.3 20.3 %collective-permute-start.26 = (f32[768,256]{1,0:T(8,128)}, f32[768,256]{1,0:T(8,128)}, u32[]{:S(2)}, u32[]{:S(2)}) collective-permute-start(f32[768,256]{1,0:T(8,128)} %fusion.51), channel_id=1, source_target_pairs={{0,16},{16,0},{1,17},{17,1},{2,18},{18,2},{3,19},{19,3},{4,20},{20... | collective-permute-start | bytes 2359304 | tf_op jit(solution)/shard_map/ppermute | solution.py:49
  390.5 29.3 %collective-permute-start.28 = (f32[2,2,2,146,256]{4,2,3,1,0:T(2,128)S(1)}, f32[2,2,2,146,256]{4,2,3,1,0:T(2,128)S(1)}, u32[]{:S(2)}, u32[]{:S(2)}) collective-permute-start(f32[2,2,2,146,256]{4,2,3,1,0:T(2,128)S(1)} %copy.222), channel_id=1, source_target_pairs={{0,1},{1,0},{2,3},{3,2},{4,5},{5,4},{6,7},{7,6},{8,9},{9,8},{10,11... | collective-permute-start | bytes 3588104 | tf_op jit(solution)/shard_map/ppermute | solution.py:49
  395.3 114.9 %collective-permute-start.36 = (f32[2,2,2,288,256]{4,3,2,1,0:T(8,128)}, f32[2,2,2,288,256]{4,3,2,1,0:T(8,128)}, u32[]{:S(2)}, u32[]{:S(2)}) collective-permute-start(f32[2,2,2,288,256]{4,3,2,1,0:T(8,128)} %slice_bitcast_fusion), channel_id=1, source_target_pairs={{0,1},{1,0},{2,3},{3,2},{4,5},{5,4},{6,7},{7,6},{8,9},{9,8},{10,11... | collective-permute-start | bytes 7077896 | tf_op jit(solution)/shard_map/ppermute | solution.py:49
  400.9 18.9 %copy-start.20 = (f32[16,146,256]{2,1,0:T(8,128)S(1)}, f32[16,146,256]{2,1,0:T(8,128)}, u32[]{:S(2)}) copy-start(f32[16,146,256]{2,1,0:T(8,128)} %gather_fusion.10) | copy-start | bytes 7176196
  402.3 82.1 %collective-permute-start.9 = (f32[2,160,512]{2,1,0:T(8,128)}, f32[2,160,512]{2,1,0:T(8,128)S(1)}, u32[]{:S(2)}, u32[]{:S(2)}) collective-permute-start(f32[2,160,512]{2,1,0:T(8,128)} %get-tuple-element.46), channel_id=1, source_target_pairs={{0,1},{1,0},{2,3},{3,2},{4,5},{5,4},{6,7},{7,6},{8,9},{9,8},{10,11... | collective-permute-start | bytes 1966088 | tf_op jit(solution)/shard_map/ppermute | solution.py:49
  403.5 93.1 %collective-permute-start.11 = (f32[2,160,512]{2,1,0:T(8,128)}, f32[2,160,512]{2,1,0:T(8,128)}, u32[]{:S(2)}, u32[]{:S(2)}) collective-permute-start(f32[2,160,512]{2,1,0:T(8,128)} %get-tuple-element.47), channel_id=1, source_target_pairs={{0,3},{1,2},{2,1},{3,0},{4,7},{5,6},{6,5},{7,4},{8,11},{9,10},{10,... | collective-permute-start | bytes 1966088 | tf_op jit(solution)/shard_map/ppermute | solution.py:49
  404.3 92.3 %collective-permute-start.10 = (f32[2,160,512]{2,1,0:T(8,128)S(1)}, f32[2,160,512]{2,1,0:T(8,128)}, u32[]{:S(2)}, u32[]{:S(2)}) collective-permute-start(f32[2,160,512]{2,1,0:T(8,128)S(1)} %get-tuple-element.48), channel_id=1, source_target_pairs={{0,2},{1,3},{2,0},{3,1},{4,6},{5,7},{6,4},{7,5},{8,10},{9,11},{10,... | collective-permute-start | bytes 1966088 | tf_op jit(solution)/shard_map/ppermute | solution.py:49
  421.2 87.9 %collective-permute-start.29 = (f32[2,2,146,256]{3,1,2,0:T(2,128)}, f32[2,2,146,256]{3,1,2,0:T(2,128)}, u32[]{:S(2)}, u32[]{:S(2)}) collective-permute-start(f32[2,2,146,256]{3,1,2,0:T(2,128)} %copy.224), channel_id=1, source_target_pairs={{0,2},{1,3},{2,0},{3,1},{4,6},{5,7},{6,4},{7,5},{8,10},{9,11},{10,... | collective-permute-start | bytes 1794056 | tf_op jit(solution)/shard_map/ppermute | solution.py:49
  509.0 37.1 %collective-permute-start.24 = (f32[160,512]{1,0:T(8,128)S(1)}, f32[160,512]{1,0:T(8,128)S(1)}, u32[]{:S(2)}, u32[]{:S(2)}) collective-permute-start(f32[160,512]{1,0:T(8,128)S(1)} %reduce_sum.250), channel_id=1, source_target_pairs={{0,16},{16,0},{1,17},{17,1},{2,18},{18,2},{3,19},{19,3},{4,20},{20... | collective-permute-start | bytes 983048 | tf_op jit(solution)/shard_map/ppermute | solution.py:49
  515.5 28.7 %collective-permute-start.37 = (f32[2,2,288,256]{3,2,1,0:T(8,128)}, f32[2,2,288,256]{3,2,1,0:T(8,128)}, u32[]{:S(2)}, u32[]{:S(2)}) collective-permute-start(f32[2,2,288,256]{3,2,1,0:T(8,128)} %slice_bitcast_fusion.10), channel_id=1, source_target_pairs={{0,2},{1,3},{2,0},{3,1},{4,6},{5,7},{6,4},{7,5},{8,10},{9,11},{10,... | collective-permute-start | bytes 3538952 | tf_op jit(solution)/shard_map/ppermute | solution.py:49
  517.7 9.8 %collective-permute-start.30 = (f32[2,146,256]{2,1,0:T(8,128)}, f32[2,146,256]{2,1,0:T(8,128)}, u32[]{:S(2)}, u32[]{:S(2)}) collective-permute-start(f32[2,146,256]{2,1,0:T(8,128)} %slice_bitcast_fusion.35), channel_id=1, source_target_pairs={{0,4},{1,5},{2,6},{3,7},{4,0},{5,1},{6,2},{7,3},{8,12},{9,13},{10,... | collective-permute-start | bytes 897032 | tf_op jit(solution)/shard_map/ppermute | solution.py:49
  528.5 19.3 %collective-permute-start.31 = (f32[146,256]{1,0:T(8,128)S(1)}, f32[146,256]{1,0:T(8,128)S(1)}, u32[]{:S(2)}, u32[]{:S(2)}) collective-permute-start(f32[146,256]{1,0:T(8,128)S(1)} %slice_bitcast_fusion.47), channel_id=1, source_target_pairs={{0,8},{1,9},{2,10},{3,11},{4,12},{5,13},{6,14},{7,15},{8,0},{9,1},... | collective-permute-start | bytes 448520 | tf_op jit(solution)/shard_map/ppermute | solution.py:49
  546.0 15.0 %collective-permute-start.38 = (f32[2,288,256]{2,1,0:T(8,128)S(1)}, f32[2,288,256]{2,1,0:T(8,128)S(1)}, u32[]{:S(2)}, u32[]{:S(2)}) collective-permute-start(f32[2,288,256]{2,1,0:T(8,128)S(1)} %slice_bitcast_fusion.31), channel_id=1, source_target_pairs={{0,4},{1,5},{2,6},{3,7},{4,0},{5,1},{6,2},{7,3},{8,12},{9,13},{10,... | collective-permute-start | bytes 1769480 | tf_op jit(solution)/shard_map/ppermute | solution.py:49
  547.8 18.0 %collective-permute-start.32 = (f32[146,256]{1,0:T(8,128)S(1)}, f32[146,256]{1,0:T(8,128)S(1)}, u32[]{:S(2)}, u32[]{:S(2)}) collective-permute-start(f32[146,256]{1,0:T(8,128)S(1)} %fusion.79), channel_id=1, source_target_pairs={{0,16},{16,0},{1,17},{17,1},{2,18},{18,2},{3,19},{19,3},{4,20},{20... | collective-permute-start | bytes 448520 | tf_op jit(solution)/shard_map/ppermute | solution.py:49
  561.8 15.2 %collective-permute-start.39 = (f32[288,256]{1,0:T(8,128)}, f32[288,256]{1,0:T(8,128)S(1)}, u32[]{:S(2)}, u32[]{:S(2)}) collective-permute-start(f32[288,256]{1,0:T(8,128)} %slice_bitcast_fusion.37), channel_id=1, source_target_pairs={{0,8},{1,9},{2,10},{3,11},{4,12},{5,13},{6,14},{7,15},{8,0},{9,1},... | collective-permute-start | bytes 884744 | tf_op jit(solution)/shard_map/ppermute | solution.py:49
  577.0 1.6 collective-permute-start.40
  (67 other events, 306.4 us)
